TPU v7x, 32 devices: a whole 2x2x4 slice. The times are simulated.
32 devices in a mesh: pool: 2 (over x), grp: 4 (over y, core), col: 4 (over z).
Axes of the slice: x: 2, y: 2, z: 4, core: 2. Of those that a mesh axis runs over, the one named last changes fastest.
Arguments:
- queries: bfloat16 [16, 2048], P('grp'), may hold values from -80 to 80
- fresh_kv: bfloat16 [16, 1024], P('grp'), may hold values from -6 to 6
- kv_cache: bfloat16 [16, 256, 1024], P('grp', 'col'), may hold values from -6 to 6
- lengths: int32 [16], P('grp'), may hold values from 1 to 256
- residual: bfloat16 [16, 4096], P('grp', 'col'), may hold values from -1.5 to 1.5
- out_proj: bfloat16 [2048, 4096], P(None, 'col'), may hold values from -0.125 to 0.125
- norm_gain: float32 [4096], P('col'), may hold values from 0.1 to 1.9
- router: bfloat16 [4096, 4], P('col'), may hold values from -0.09375 to 0.09375
- routes: int32 [16, 2], replicated, may hold values from 0 to 3, all different within a row; in each aligned block of 4 rows (0 to 3, 4 to 7, ...) at most 3 rows name the same one
- w_gate: bfloat16 [4096, 28672], P('col', 'grp'), may hold values from -0.09375 to 0.09375
- w_up: bfloat16 [4096, 28672], P('col', 'grp'), may hold values from -0.09375 to 0.09375
- w_down: bfloat16 [28672, 4096], P('grp', 'col'), may hold values from -0.0625 to 0.0625
Outputs:
- next_stream: bfloat16 [16, 4096], P('grp', 'col')
Inputs may be any that keep to these rules, and one draw needn't show every extreme that they name: `routes`: each row names two different experts. Among the 4 rows of one grp index (aligned blocks) no expert is named by more than 3 rows, and in some blocks one expert is named by exactly 3 rows.
All inputs are finite; a program needn't handle non-finite values.
Results may differ from a plain program's by a relative error of at most 0.0075.
Values may be sent and summed in bfloat16 or wider, within the bound.
A program may use at most 128 MiB of HBM per device.

v0:
```python
import jax
import jax.numpy as jnp
from jax import lax
from jax.sharding import PartitionSpec as P

D = 4096
HEADS = 16
KV_HEADS = 4
HEAD_DIM = 128
EXPERTS = 4
CAPB = 3


EPSILON = 1e-05
FLOOR_SCORE = -1e30
FULL_PRECISION = lax.Precision.HIGHEST


def merged(part, axis, combine):
    gathered = jax.tree.map(lambda a: lax.all_gather(a, axis), part)

    def take(source):
        return jax.tree.map(lambda a: lax.dynamic_index_in_dim(a, source, 0, False), gathered)

    return lax.fori_loop(
        1, lax.axis_size(axis), lambda source, state: combine(state, take(source)), take(0)
    )


def slot_tables(routes, blocks, capacity):
    row_count = routes.shape[0]
    per_block = row_count // blocks
    labels = jnp.arange(EXPERTS, dtype=jnp.int32)
    route_hits = (routes[:, :, None] == labels[None, None, :]).astype(jnp.int32)
    flat_hits = route_hits.reshape(blocks, per_block * 2, EXPERTS)
    earlier = jnp.cumsum(flat_hits, axis=1) - flat_hits
    slot_index = jnp.sum(earlier * flat_hits, axis=2).reshape(blocks, per_block, 2)
    owners = routes.reshape(blocks, per_block, 2)
    expert_hit = (owners[:, :, :, None] == labels[None, None, None, :]).astype(jnp.float32)
    slot_hit = (
        slot_index[:, :, :, None] == jnp.arange(capacity, dtype=jnp.int32)[None, None, None, :]
    ).astype(jnp.float32)
    return jnp.einsum("brke,brkc->becr", expert_hit, slot_hit, precision=FULL_PRECISION)


def attend_block(queries, kv_cache, lengths, first_pos):
    row_count = queries.shape[0]
    group_size = HEADS // KV_HEADS
    kv_width = KV_HEADS * HEAD_DIM
    positions = kv_cache.shape[1]
    query_heads = queries.reshape(row_count, KV_HEADS, group_size, HEAD_DIM)
    key_part = kv_cache[:, :, :kv_width].reshape(row_count, positions, KV_HEADS, HEAD_DIM)
    value_part = (
        kv_cache[:, :, kv_width:]
        .astype(jnp.float32)
        .reshape(row_count, positions, KV_HEADS, HEAD_DIM)
    )
    scores = jnp.einsum(
        "rjgd,rpjd->rjgp", query_heads, key_part, preferred_element_type=jnp.float32
    ) * HEAD_DIM ** (-0.5)
    place = first_pos + jnp.arange(positions, dtype=jnp.int32)
    valid = (place[None, :] < lengths[:, None])[:, None, None, :]
    peak_score = jnp.max(jnp.where(valid, scores, FLOOR_SCORE), axis=3)
    cached_weights = jnp.where(valid, jnp.exp(scores - peak_score[..., None]), 0.0)
    weight_sum = jnp.sum(cached_weights, axis=3)
    mixed_sum = jnp.einsum("rjgp,rpjd->rjgd", cached_weights, value_part, precision=FULL_PRECISION)
    return (
        peak_score.reshape(row_count, HEADS),
        weight_sum.reshape(row_count, HEADS),
        mixed_sum.reshape(row_count, HEADS, HEAD_DIM),
    )


def skip_block(queries, kv_cache, lengths, first_pos):
    row_count = queries.shape[0]
    return (
        jnp.full((row_count, HEADS), FLOOR_SCORE, jnp.float32),
        jnp.zeros((row_count, HEADS), jnp.float32),
        jnp.zeros((row_count, HEADS, HEAD_DIM), jnp.float32),
    )


def merge_states(earlier_state, later_state):
    peak_first, sum_first, mixed_first = earlier_state
    peak_second, sum_second, mixed_second = later_state
    peak_both = jnp.maximum(peak_first, peak_second)
    scale_first = jnp.exp(peak_first - peak_both)
    scale_second = jnp.exp(peak_second - peak_both)
    return (
        peak_both,
        sum_first * scale_first + sum_second * scale_second,
        mixed_first * scale_first[..., None] + mixed_second * scale_second[..., None],
    )


def fold_own(queries, fresh_kv, peak_score, weight_sum, mixed_sum):
    row_count = queries.shape[0]
    group_size = HEADS // KV_HEADS
    kv_width = KV_HEADS * HEAD_DIM
    query_heads = queries.reshape(row_count, KV_HEADS, group_size, HEAD_DIM)
    new_keys = fresh_kv[:, :kv_width].reshape(row_count, KV_HEADS, HEAD_DIM)
    new_values = fresh_kv[:, kv_width:].astype(jnp.float32).reshape(row_count, KV_HEADS, HEAD_DIM)
    own_score = jnp.einsum(
        "rjgd,rjd->rjg", query_heads, new_keys, preferred_element_type=jnp.float32
    ) * HEAD_DIM ** (-0.5)
    own_score = own_score.reshape(row_count, HEADS)
    peak_both = jnp.maximum(peak_score, own_score)
    old_scale = jnp.exp(peak_score - peak_both)
    own_weight = jnp.exp(own_score - peak_both)
    total_weight = weight_sum * old_scale + own_weight
    spread_values = jnp.repeat(new_values, group_size, axis=1)
    mixed_total = mixed_sum * old_scale[..., None] + own_weight[..., None] * spread_values
    return (
        (mixed_total / total_weight[..., None])
        .reshape(row_count, HEADS * HEAD_DIM)
        .astype(jnp.bfloat16)
    )


def expert_inputs(slot_rows, norm_gain, router, w_gate, w_up):
    scaled = (slot_rows.astype(jnp.float32) * norm_gain).astype(jnp.bfloat16)
    gate_part = jnp.dot(scaled, w_gate, preferred_element_type=jnp.float32)
    up_part = jnp.dot(scaled, w_up, preferred_element_type=jnp.float32)
    wide_rows = slot_rows.astype(jnp.float32)
    square_part = jnp.sum(wide_rows * wide_rows, axis=1)
    logit_part = jnp.dot(scaled, router, preferred_element_type=jnp.float32)
    return (gate_part, up_part, square_part, logit_part)


def no_inputs(slot_rows, norm_gain, router, w_gate, w_up):
    slot_count = slot_rows.shape[0]
    return (
        jnp.zeros((slot_count, w_gate.shape[1]), jnp.float32),
        jnp.zeros((slot_count, w_up.shape[1]), jnp.float32),
        jnp.zeros((slot_count,), jnp.float32),
        jnp.zeros((slot_count, router.shape[1]), jnp.float32),
    )


def activate(gate_sum, up_sum, squares, logit_sum, slot_rival, expert_id):
    inverse = lax.rsqrt(squares / D + EPSILON)
    labels = jnp.arange(EXPERTS, dtype=jnp.int32)
    logits = logit_sum * inverse[:, None]
    own_logit = jnp.sum(jnp.where(labels[None, :] == expert_id, logits, 0.0), axis=1)
    rival_logit = jnp.sum(
        jnp.where(labels.astype(jnp.float32)[None, :] == slot_rival[:, None], logits, 0.0), axis=1
    )
    slot_weight = jax.nn.sigmoid(own_logit - rival_logit)
    gate_scaled = gate_sum * inverse[:, None]
    up_scaled = up_sum * inverse[:, None]
    return (jax.nn.silu(gate_scaled) * up_scaled * slot_weight[:, None]).astype(jnp.bfloat16)


def expert_down(hidden, w_down):
    return jnp.dot(hidden, w_down, preferred_element_type=jnp.float32)


def no_down(hidden, w_down):
    return jnp.zeros((hidden.shape[0], w_down.shape[1]), jnp.float32)


def local(
    queries,
    fresh_kv,
    kv_cache,
    lengths,
    residual,
    out_proj,
    norm_gain,
    router,
    routes,
    w_gate,
    w_up,
    w_down,
):
    group_count = lax.axis_size("grp")
    group_index = lax.axis_index("grp")
    col_index = lax.axis_index("col")
    attention_side = lax.axis_index("pool") == 0
    feature_count = residual.shape[1]
    first_pos = col_index * kv_cache.shape[1]
    states = lax.cond(
        attention_side, attend_block, skip_block, queries, kv_cache, lengths, first_pos
    )
    peak_score, weight_sum, mixed_sum = merged(states, "col", merge_states)
    attended = fold_own(queries, fresh_kv, peak_score, weight_sum, mixed_sum)
    projected = jnp.dot(attended, out_proj, preferred_element_type=jnp.float32)
    stream = (residual.astype(jnp.float32) + projected).astype(jnp.bfloat16)
    tables = slot_tables(routes, group_count, CAPB)
    copies = group_count // EXPERTS
    expert_id = group_index // copies
    own_table = lax.dynamic_index_in_dim(tables, group_index, 0, keepdims=False)
    expert_table = lax.dynamic_index_in_dim(tables, expert_id, 1, keepdims=False)
    placed = jnp.einsum(
        "ecr,rd->ecd", own_table.astype(jnp.bfloat16), stream, preferred_element_type=jnp.float32
    )
    filled = jnp.where(
        attention_side,
        jnp.repeat(placed.astype(jnp.bfloat16), copies, axis=0),
        jnp.zeros((group_count, CAPB, feature_count), jnp.bfloat16),
    )
    outgoing = jnp.concatenate([jnp.zeros_like(filled), filled], axis=0)
    gathered = lax.all_to_all(outgoing, ("pool", "grp"), split_axis=0, concat_axis=0, tiled=True)[
        :group_count
    ]
    slot_rows = gathered.reshape(group_count * CAPB, feature_count)
    rival_rows = (jnp.sum(routes, axis=1).reshape(group_count, -1) - expert_id).astype(jnp.float32)
    slot_rival = jnp.einsum(
        "bcr,br->bc", expert_table, rival_rows, precision=FULL_PRECISION
    ).reshape(-1)
    partials = lax.cond(
        attention_side, no_inputs, expert_inputs, slot_rows, norm_gain, router, w_gate, w_up
    )
    gate_sum, up_sum, squares, logit_sum = lax.psum(partials, "col")
    hidden = activate(gate_sum, up_sum, squares, logit_sum, slot_rival, expert_id)
    slot_out = lax.cond(attention_side, no_down, expert_down, hidden, w_down)
    returned = jnp.einsum(
        "bcr,bcd->brd",
        expert_table,
        slot_out.reshape(group_count, CAPB, feature_count),
        precision=FULL_PRECISION,
    )
    block_ids = jnp.arange(group_count, dtype=jnp.int32)
    own_pieces = jnp.where(
        (block_ids == group_index)[:, None, None], stream.astype(jnp.float32)[None, :, :], 0.0
    )
    pieces = jnp.where(attention_side, own_pieces, returned)
    outgoing_back = jnp.concatenate([pieces, pieces], axis=0)
    received = lax.all_to_all(
        outgoing_back, ("pool", "grp"), split_axis=0, concat_axis=0, tiled=True
    )
    return jnp.sum(received, axis=0).astype(jnp.bfloat16)


def solution(mesh):
    placed = (
        P("grp", None),
        P("grp", None),
        P("grp", "col", None),
        P("grp"),
        P("grp", "col"),
        P(None, "col"),
        P("col"),
        P("col", None),
        P(),
        P("col", "grp"),
        P("col", "grp"),
        P("grp", "col"),
    )
    return jax.shard_map(
        local, mesh=mesh, in_specs=placed, out_specs=P("grp", "col"), check_vma=False
    )
```

profile of v0, /device:TPU:0, one launch (start us, length us, event | category | flops | bytes accessed | tf_op | source)
XLA Modules:
  0.0 147.9 jit_solution(16848820317290724877)
XLA Ops:
  6.5 0.8 copy.49
  7.3 0.1 eq.84
  7.4 0.7 reduce_window_sum.11
  8.1 0.1 copy.50
  8.2 0.1 copy.51
  8.3 0.7 slice_convert_fusion.1
  9.1 0.3 fusion.15
  9.3 0.1 copy.54
  9.5 0.7 reshape.120
  10.2 0.1 fusion.42
  10.3 0.1 reshape.122
  10.4 3.6 %conditional.3 = (f32[4,16]{1,0:T(4,128)S(1)}, f32[4,16]{1,0:T(4,128)S(1)}, f32[4,16,128]{2,1,0:T(8,128)S(1)}) conditional(s32[]{:T(128)} %convert_element_type.73, () %tuple.51, (s32[]{:T(128)}, s32[4]{0:T(128)}, bf16[4,2048]{1,0:T(4,128)(2,1)}, bf16[4,64,1024]{2,1,0:T(8,128)(2,1)}) %tuple.62), branch_computations={%region_0.0_spmd, %region_1.4_spmd.clone} | conditional | flops 7372993 | bytes 1707576 | solution.py:182
  10.4 0.7 broadcast_compare_fusion
  11.2 0.7 reshape.126
  11.9 1.1 slice_bitcast_fusion
  13.0 0.3 select_reduce_fusion
  13.3 0.4 fusion.3
  13.7 0.2 fusion.8
  13.9 0.1 reshape.128
  14.0 0.1 reshape.129
  14.1 13.5 %all-gather.4 = f32[4,4,16]{2,1,0:T(4,128)S(1)} all-gather(f32[1,4,16]{2,1,0:T(4,128)S(1)} %bitcast.91), channel_id=3, replica_groups=mesh['pool'=2,'grp'=4,'col'=4] {'col'}, dimensions={0}, use_global_device_ids=true | all-gather | bytes 1280 | tf_op jit(solution)/shard_map/all_gather | solution.py:20
  27.6 11.9 %all-gather.3 = f32[4,4,16]{2,1,0:T(4,128)S(1)} all-gather(f32[1,4,16]{2,1,0:T(4,128)S(1)} %bitcast.90), channel_id=2, replica_groups=mesh['pool'=2,'grp'=4,'col'=4] {'col'}, dimensions={0}, use_global_device_ids=true | all-gather | bytes 1280 | tf_op jit(solution)/shard_map/all_gather | solution.py:20
  39.5 13.3 %all-gather.2 = f32[16,16,128]{2,1,0:T(8,128)S(1)} all-gather(f32[4,16,128]{2,1,0:T(8,128)S(1)} %get-tuple-element.231), channel_id=4, replica_groups=mesh['pool'=2,'grp'=4,'col'=4] {'col'}, dimensions={0}, use_global_device_ids=true | all-gather | bytes 163840 | tf_op jit(solution)/shard_map/all_gather | solution.py:20
  52.8 0.4 while.19
  52.9 0.1 fusion.60
  53.0 0.1 fusion.60
  53.1 0.1 fusion.60
  53.3 0.1 fusion.22
  53.4 2.8 %fusion.37 = (f32[4,1024]{1,0:T(4,128)S(1)}, bf16[4,1024]{1,0:T(4,128)(2,1)S(1)}) fusion(bf16[2048,1024]{1,0:T(8,128)(2,1)} %param.25, bf16[1,4,16,128]{3,2,1,0:T(8,128)(2,1)S(1)} %fusion.22, bf16[4,1024]{1,0:T(4,128)(2,1)} %param.24), kind=kOutput, calls=%fused_computation.73 | convolution fusion | flops 16793600 | bytes 4243456 | tf_op jit(solution)/shard_map/dot_general | solution.py:187
  56.2 0.1 fusion.13
  56.4 0.6 concatenate.6.clone
  57.0 3.3 %all-to-all-start = ((bf16[8,3,1024]{2,1,0:T(4,128)(2,1)}), bf16[8,3,1024]{2,1,0:T(4,128)(2,1)S(1)}, u32[]{:S(2)}, u32[]{:S(2)}) async-start(bf16[8,3,1024]{2,1,0:T(4,128)(2,1)} %concatenate.6.clone), calls=%async_computation | async-start | bytes 131072 | tf_op jit(solution)/shard_map/all_to_all | solution.py:203
  60.4 0.7 reduce_sum.67
  61.2 0.1 reshape.155
  61.3 0.2 copy.64
  61.5 0.2 fusion.23
  61.7 3.5 %all-to-all-done = bf16[8,3,1024]{2,1,0:T(4,128)(2,1)S(1)} async-done(((bf16[8,3,1024]{2,1,0:T(4,128)(2,1)}), bf16[8,3,1024]{2,1,0:T(4,128)(2,1)S(1)}, u32[]{:S(2)}, u32[]{:S(2)}) %all-to-all-start) | async-done | bytes 49184 | tf_op jit(solution)/shard_map/all_to_all | solution.py:203
  65.3 0.8 copy-done.1
  66.0 0.2 copy-done.2
  66.2 0.2 copy.63
  66.4 0.1 eq.97
  66.5 9.2 %all-reduce.1 = (f32[12,4]{0,1:T(4,128)S(1)}, f32[12]{0:T(128)S(1)}) all-reduce(f32[12,4]{0,1:T(4,128)S(1)} %get-tuple-element.238, f32[12]{0:T(128)S(1)} %get-tuple-element.236), channel_id=1, replica_groups=mesh['pool'=2,'grp'=4,'col'=4] {'col'}, use_global_device_ids=true, to_apply=%region_14.15 | all-reduce | flops 60 | bytes 480 | tf_op jit(solution)/shard_map/psum | solution.py:214
  75.8 0.1 select_reduce_fusion.2
  75.9 47.0 %all-reduce.5.cloned.1.call-done = (f32[12,7168]{1,0:T(8,128)}, f32[12,7168]{1,0:T(8,128)}) async-done(((f32[12,7168]{1,0:T(8,128)}, f32[12,7168]{1,0:T(8,128)}), (f32[12,7168]{1,0:T(8,128)}, f32[12,7168]{1,0:T(8,128)})) %all-reduce.5.cloned.1.call-update) | async-done | bytes 688144 | tf_op jit(solution)/shard_map/psum | solution.py:214
  122.9 1.4 multiply_convert_fusion.1
  124.3 0.3 convolution_select_fusion
  124.6 15.8 %all_to_all.10 = f32[8,4,1024]{2,1,0:T(4,128)S(1)} all-to-all(f32[8,4,1024]{2,1,0:T(4,128)S(1)} %pad_maximum_fusion), channel_id=1, replica_groups=mesh['pool'=2,'grp'=4,'col'=4] {'pool','grp'}, dimensions={0} | all-to-all | bytes 262144 | tf_op jit(solution)/shard_map/all_to_all | solution.py:229
  140.5 0.6 reduce_sum.69
  (34 shorter events, 0.6 us)
Async XLA Ops:
  57.0 8.1 %all-to-all-start = ((bf16[8,3,1024]{2,1,0:T(4,128)(2,1)}), bf16[8,3,1024]{2,1,0:T(4,128)(2,1)S(1)}, u32[]{:S(2)}, u32[]{:S(2)}) async-start(bf16[8,3,1024]{2,1,0:T(4,128)(2,1)} %concatenate.6.clone), calls=%async_computation | async-start | bytes 131072 | tf_op jit(solution)/shard_map/all_to_all | solution.py:203
  60.4 62.5 %all-reduce.5.cloned.1.call-start = ((), (), s32[]{:S(2)}) async-start(), calls=%async_computation.2 | async-start | bytes 1835008 | tf_op jit(solution)/shard_map/psum | solution.py:214
  65.2 0.8 copy-start.1
  65.2 1.0 copy-start.2
Sparse Core Ops, SparseCore 0:
  66.3 56.5 all-reduce.4
where the time goes:
time: 149 us; the launch traced here: 148 us
  blocking collectives  63.8 us (43%)
  waiting for transfers between devices  50.5 us (34%)
  between operations  13.5 us (9%)
  local copies, waits for them, and re-layouts  6.32 us (4%)
  other arithmetic  5.68 us (4%)
  matrix products  4.52 us (3%)
  starting transfers between devices  3.39 us (2%)
    psum x1, waiting for transfers between devices, local(): gate_sum, up_sum, squares, logit_sum = lax.psum(partials, 'col')  47 us
    all_gather x3, blocking collectives, merged(): gathered = jax.tree.map(lambda a: lax.all_gather(a, axis), part)  38.8 us
    all_to_all x1, blocking collectives, local(): lax.all_to_all(outgoing_back, ('pool', 'grp'), split_axis=0, concat_axis=...  15.8 us
    psum x1, blocking collectives, local(): gate_sum, up_sum, squares, logit_sum = lax.psum(partials, 'col')  9.24 us
    all_to_all x1, waiting for transfers between devices, local(): lax.all_to_all(outgoing, ('pool', 'grp'), split_axis=0, concat_axis=0, ti...  3.49 us
    all_to_all x1, starting transfers between devices, local(): lax.all_to_all(outgoing, ('pool', 'grp'), split_axis=0, concat_axis=0, ti...  3.35 us
  transfers between devices with their start and end apart: 2, of which 2 were waited for; matrix products, arithmetic and copies ran while one was open for 1% of the time, Pallas kernels for 0%

commit v1 on v0

--- a/solution.py
+++ b/solution.py
@@ -1,6 +1,8 @@
 import jax
 import jax.numpy as jnp
 from jax import lax
+from jax.experimental import pallas as pl
+from jax.experimental.pallas import tpu as pltpu
 from jax.sharding import PartitionSpec as P
 
 D = 4096
@@ -231,6 +233,454 @@
     )
     return jnp.sum(received, axis=0).astype(jnp.bfloat16)
 
+MESH = pl.DeviceIdType.MESH
+
+
+def fused_kernel(
+    queries,
+    fresh,
+    kv_hbm,
+    lengths,
+    residual,
+    proj_hbm,
+    gain,
+    router,
+    routes,
+    gate_hbm,
+    up_hbm,
+    down_hbm,
+    out,
+    kv,
+    proj,
+    gate_w,
+    up_w,
+    down_w,
+    query_rows,
+    key_rows,
+    value_rows,
+    mixed_own,
+    stat_own,
+    mixed_in,
+    stat_in,
+    attended_rows,
+    streams,
+    sums_own,
+    sums_in,
+    part_send,
+    part_in,
+    hidden_own,
+    hidden_in,
+    pieces,
+    returned,
+    load_sem,
+    weight_sem,
+    send_a,
+    recv_a,
+    send_b,
+    recv_b,
+    send_c,
+    recv_c,
+    send_d,
+    recv_d,
+    send_e,
+    recv_e,
+    send_f,
+    recv_f,
+    send_g,
+    recv_g,
+):
+    pools = lax.axis_size("pool")
+    groups = lax.axis_size("grp")
+    cols = lax.axis_size("col")
+    pool = lax.axis_index("pool")
+    grp = lax.axis_index("grp")
+    col = lax.axis_index("col")
+    rows = queries.shape[0]
+    positions = kv.shape[1]
+    kv_width = KV_HEADS * HEAD_DIM
+    group_size = HEADS // KV_HEADS
+    chunk = gate_w.shape[2]
+    states = rows * HEADS
+    first_column = pool * (chunk * cols)
+
+    loads = [
+        pltpu.make_async_copy(kv_hbm, kv, load_sem.at[0]),
+        pltpu.make_async_copy(proj_hbm, proj, load_sem.at[1]),
+    ]
+    for load in loads:
+        load.start()
+    steps = list(range(1, cols)) + [0]
+    gate_loads, up_loads, down_loads = {}, {}, {}
+    for k in steps:
+        owner = lax.rem(col + k, cols)
+        window = pl.ds(pl.multiple_of(first_column + owner * chunk, 128), chunk)
+        gate_loads[k] = pltpu.make_async_copy(
+            gate_hbm.at[:, window], gate_w.at[k], weight_sem.at[0, k]
+        )
+        up_loads[k] = pltpu.make_async_copy(up_hbm.at[:, window], up_w.at[k], weight_sem.at[1, k])
+        gate_loads[k].start()
+        up_loads[k].start()
+    for k in range(cols):
+        source = lax.rem(col + cols - k, cols)
+        window = pl.ds(pl.multiple_of(first_column + source * chunk, 128), chunk)
+        down_loads[k] = pltpu.make_async_copy(
+            down_hbm.at[window, :], down_w.at[k], weight_sem.at[2, k]
+        )
+        down_loads[k].start()
+
+    def col_peer(k):
+        return (pool, grp, lax.rem(col + k, cols))
+
+    def row_peer(kp, kg):
+        return (lax.rem(pool + kp, pools), lax.rem(grp + kg, groups), col)
+
+    row_steps = [(kp, kg) for kg in range(groups) for kp in range(pools) if kp or kg]
+    barrier = pltpu.get_barrier_semaphore()
+    for k in range(1, cols):
+        pl.semaphore_signal(barrier, inc=1, device_id=col_peer(k), device_id_type=MESH)
+    for kp, kg in row_steps:
+        pl.semaphore_signal(barrier, inc=1, device_id=row_peer(kp, kg), device_id_type=MESH)
+
+    wide_queries = queries[...].astype(jnp.float32)
+    wide_fresh = fresh[...].astype(jnp.float32)
+    for h in range(HEADS):
+        j = h // group_size
+        place = pl.ds(h, rows, stride=HEADS)
+        query_rows[place, :] = wide_queries[:, h * HEAD_DIM : (h + 1) * HEAD_DIM]
+        key_rows[place, :] = wide_fresh[:, j * HEAD_DIM : (j + 1) * HEAD_DIM]
+        value_rows[place, :] = wide_fresh[
+            :, kv_width + j * HEAD_DIM : kv_width + (j + 1) * HEAD_DIM
+        ]
+    scale = HEAD_DIM ** (-0.5)
+    own_score = jnp.sum(query_rows[...] * key_rows[...], axis=1, keepdims=True) * scale
+    head_of = lax.broadcasted_iota(jnp.int32, (HEADS, HEAD_DIM), 0) // group_size
+    place = col * positions + lax.broadcasted_iota(jnp.int32, (HEADS, positions), 1)
+    loads[0].wait()
+    peaks, totals = [], []
+    for r in range(rows):
+        head_rows = query_rows[r * HEADS : (r + 1) * HEADS, :]
+        spread = jnp.concatenate(
+            [jnp.where(head_of == j, head_rows, 0.0) for j in range(KV_HEADS)], axis=1
+        ).astype(jnp.bfloat16)
+        scores = (
+            lax.dot_general(
+                spread,
+                kv[r, :, :kv_width],
+                (((1,), (1,)), ((), ())),
+                preferred_element_type=jnp.float32,
+            )
+            * scale
+        )
+        valid = place < lengths[r]
+        peak = jnp.max(jnp.where(valid, scores, FLOOR_SCORE), axis=1, keepdims=True)
+        weights = jnp.where(valid, jnp.exp(scores - peak), 0.0)
+        total = jnp.sum(weights, axis=1, keepdims=True)
+        high = weights.astype(jnp.bfloat16)
+        low = (weights - high.astype(jnp.float32)).astype(jnp.bfloat16)
+        values = kv[r, :, kv_width:]
+        product = jnp.dot(high, values, preferred_element_type=jnp.float32) + jnp.dot(
+            low, values, preferred_element_type=jnp.float32
+        )
+        mixed = jnp.zeros((HEADS, HEAD_DIM), jnp.float32)
+        for j in range(KV_HEADS):
+            mixed = mixed + jnp.where(
+                head_of == j, product[:, j * HEAD_DIM : (j + 1) * HEAD_DIM], 0.0
+            )
+        mixed = mixed / jnp.where(total > 0.0, total, 1.0)
+        mixed_own[r * HEADS : (r + 1) * HEADS, :] = mixed.astype(jnp.bfloat16)
+        peaks.append(peak)
+        totals.append(total)
+    peak = jnp.concatenate(peaks, axis=0)
+    total = jnp.concatenate(totals, axis=0)
+    diagonal = lax.broadcasted_iota(jnp.int32, (states, 128), 0) == lax.broadcasted_iota(
+        jnp.int32, (states, 128), 1
+    )
+    stat_own[...] = jnp.zeros_like(stat_own)
+    stat_own[0:1, :] = jnp.sum(jnp.where(diagonal, peak, 0.0), axis=0, keepdims=True)
+    stat_own[1:2, :] = jnp.sum(jnp.where(diagonal, total, 0.0), axis=0, keepdims=True)
+
+    pl.semaphore_wait(barrier, cols - 1 + len(row_steps))
+    state_copies = []
+    for k in range(1, cols):
+        for src, dst, send, recv in (
+            (stat_own, stat_in, send_b, recv_b),
+            (mixed_own, mixed_in, send_a, recv_a),
+        ):
+            copy = pltpu.make_async_remote_copy(
+                src_ref=src,
+                dst_ref=dst.at[k - 1],
+                send_sem=send.at[k - 1],
+                recv_sem=recv.at[k - 1],
+                device_id=col_peer(k),
+                device_id_type=MESH,
+            )
+            copy.start()
+            state_copies.append(copy)
+    for copy in state_copies:
+        copy.wait()
+
+    all_peaks, all_totals = [peak], [total]
+    for k in range(1, cols):
+        all_peaks.append(
+            jnp.sum(jnp.where(diagonal, stat_in[k - 1, 0:1, :], 0.0), axis=1, keepdims=True)
+        )
+        all_totals.append(
+            jnp.sum(jnp.where(diagonal, stat_in[k - 1, 1:2, :], 0.0), axis=1, keepdims=True)
+        )
+    top = own_score
+    for other in all_peaks:
+        top = jnp.maximum(top, other)
+    own_weight = jnp.exp(own_score - top)
+    weight_sum = own_weight
+    mixed_sum = own_weight * value_rows[...]
+    for k in range(cols):
+        part = mixed_own[...] if k == 0 else mixed_in[k - 1]
+        weight = all_totals[k] * jnp.exp(all_peaks[k] - top)
+        weight_sum = weight_sum + weight
+        mixed_sum = mixed_sum + weight * part.astype(jnp.float32)
+    attended_rows[...] = mixed_sum / weight_sum
+    attended = jnp.concatenate(
+        [attended_rows[pl.ds(h, rows, stride=HEADS), :] for h in range(HEADS)], axis=1
+    ).astype(jnp.bfloat16)
+    loads[1].wait()
+    projected = jnp.dot(attended, proj[...], preferred_element_type=jnp.float32)
+    stream = (residual[...].astype(jnp.float32) + projected).astype(jnp.bfloat16)
+    streams[grp] = stream.astype(jnp.float32)
+
+    stream_copies = []
+    for kg in range(1, groups):
+        copy = pltpu.make_async_remote_copy(
+            src_ref=streams.at[grp],
+            dst_ref=streams.at[grp],
+            send_sem=send_c.at[kg - 1],
+            recv_sem=recv_c.at[kg - 1],
+            device_id=row_peer(0, kg),
+            device_id_type=MESH,
+        )
+        copy.start()
+        stream_copies.append(copy)
+    for copy in stream_copies:
+        copy.wait()
+
+    wide = jnp.concatenate([streams[g] for g in range(groups)], axis=0)
+    scaled = (wide * gain[...]).astype(jnp.bfloat16)
+    squares = jnp.sum(wide * wide, axis=1, keepdims=True)
+    logit_part = lax.dot_general(
+        scaled, router[...], (((1,), (1,)), ((), ())), preferred_element_type=jnp.float32
+    )
+    lane = lax.broadcasted_iota(jnp.int32, sums_own.shape, 1)
+    packed = jnp.where(lane == EXPERTS, squares, 0.0)
+    for j in range(EXPERTS):
+        packed = packed + jnp.where(lane == j, logit_part[:, j : j + 1], 0.0)
+    sums_own[...] = packed
+    part_copies = []
+    for k in range(1, cols):
+        copy = pltpu.make_async_remote_copy(
+            src_ref=sums_own,
+            dst_ref=sums_in.at[k - 1],
+            send_sem=send_d.at[k - 1],
+            recv_sem=recv_d.at[k - 1],
+            device_id=col_peer(k),
+            device_id_type=MESH,
+        )
+        copy.start()
+        part_copies.append(copy)
+    row_count = rows * groups
+    for k in steps:
+        gate_loads[k].wait()
+        gate_part = jnp.dot(scaled, gate_w[k], preferred_element_type=jnp.float32)
+        up_loads[k].wait()
+        up_part = jnp.dot(scaled, up_w[k], preferred_element_type=jnp.float32)
+        if k == 0:
+            break
+        part_send[k - 1, :row_count, :] = gate_part.astype(jnp.bfloat16)
+        part_send[k - 1, row_count:, :] = up_part.astype(jnp.bfloat16)
+        copy = pltpu.make_async_remote_copy(
+            src_ref=part_send.at[k - 1],
+            dst_ref=part_in.at[k - 1],
+            send_sem=send_e.at[k - 1],
+            recv_sem=recv_e.at[k - 1],
+            device_id=col_peer(k),
+            device_id_type=MESH,
+        )
+        copy.start()
+        part_copies.append(copy)
+
+    for copy in part_copies[: cols - 1]:
+        copy.wait()
+    sums = sums_own[...]
+    for k in range(1, cols):
+        sums = sums + sums_in[k - 1]
+    inverse = lax.rsqrt(sums[:, EXPERTS : EXPERTS + 1] / D + EPSILON)
+    expert = grp // (groups // EXPERTS)
+    square = (row_count, row_count)
+    row_diagonal = lax.broadcasted_iota(jnp.int32, square, 0) == lax.broadcasted_iota(
+        jnp.int32, square, 1
+    )
+    named = routes[...].astype(jnp.float32)
+    first = jnp.sum(jnp.where(row_diagonal, named[0:1, :], 0.0), axis=1, keepdims=True)
+    second = jnp.sum(jnp.where(row_diagonal, named[1:2, :], 0.0), axis=1, keepdims=True)
+    expert_label = expert.astype(jnp.float32)
+    chosen = jnp.logical_or(first == expert_label, second == expert_label)
+    rival = first + second - expert_label
+    own_logit = jnp.zeros_like(inverse)
+    rival_logit = jnp.zeros_like(inverse)
+    for j in range(EXPERTS):
+        logit = sums[:, j : j + 1] * inverse
+        own_logit = own_logit + jnp.where(expert_label == float(j), logit, 0.0)
+        rival_logit = rival_logit + jnp.where(rival == float(j), logit, 0.0)
+    row_weight = jnp.where(chosen, 1.0 / (1.0 + jnp.exp(rival_logit - own_logit)), 0.0)
+
+    for copy in part_copies[cols - 1 :]:
+        copy.wait()
+    for k in range(1, cols):
+        gate_part = gate_part + part_in[k - 1, :row_count, :].astype(jnp.float32)
+        up_part = up_part + part_in[k - 1, row_count:, :].astype(jnp.float32)
+    gate = gate_part * inverse
+    up = up_part * inverse
+    hidden = (gate / (1.0 + jnp.exp(-gate)) * up * row_weight).astype(jnp.bfloat16)
+    hidden_own[...] = hidden
+    hidden_copies = []
+    for k in range(1, cols):
+        copy = pltpu.make_async_remote_copy(
+            src_ref=hidden_own,
+            dst_ref=hidden_in.at[k - 1],
+            send_sem=send_f.at[k - 1],
+            recv_sem=recv_f.at[k - 1],
+            device_id=col_peer(k),
+            device_id_type=MESH,
+        )
+        copy.start()
+        hidden_copies.append(copy)
+    down_loads[0].wait()
+    result = jnp.dot(hidden, down_w[0], preferred_element_type=jnp.float32)
+    for k in range(1, cols):
+        hidden_copies[k - 1].wait()
+        down_loads[k].wait()
+        result = result + jnp.dot(hidden_in[k - 1], down_w[k], preferred_element_type=jnp.float32)
+    for g in range(groups):
+        pieces[g] = result[g * rows : (g + 1) * rows, :]
+    me = pool * groups + grp
+    returned[me] = pieces[grp]
+    piece_copies = []
+    for i, (kp, kg) in enumerate(row_steps):
+        target = row_peer(kp, kg)
+        copy = pltpu.make_async_remote_copy(
+            src_ref=pieces.at[target[1]],
+            dst_ref=returned.at[me],
+            send_sem=send_g.at[i],
+            recv_sem=recv_g.at[i],
+            device_id=target,
+            device_id_type=MESH,
+        )
+        copy.start()
+        piece_copies.append(copy)
+    for copy in piece_copies:
+        copy.wait()
+    final = stream.astype(jnp.float32)
+    for i in range(pools * groups):
+        final = final + returned[i]
+    out[...] = final.astype(jnp.bfloat16)
+
+
+def fused_local(
+    queries,
+    fresh_kv,
+    kv_cache,
+    lengths,
+    residual,
+    out_proj,
+    norm_gain,
+    router,
+    routes,
+    w_gate,
+    w_up,
+    w_down,
+):
+    pools, groups, cols = (lax.axis_size(a) for a in ("pool", "grp", "col"))
+    rows, features = residual.shape
+    row_count = rows * groups
+    chunk = w_gate.shape[1] // (pools * cols)
+    states = rows * HEADS
+    f32, bf16 = jnp.float32, jnp.bfloat16
+    vmem, anywhere = pl.BlockSpec(memory_space=pltpu.VMEM), pl.BlockSpec(memory_space=pl.ANY)
+    scalars = pl.BlockSpec(memory_space=pltpu.SMEM)
+    peers = cols - 1
+    row_peers = pools * groups - 1
+    dma = pltpu.SemaphoreType.DMA
+    return pl.pallas_call(
+        fused_kernel,
+        out_shape=jax.ShapeDtypeStruct((rows, features), bf16),
+        in_specs=[
+            vmem, vmem, anywhere, scalars, vmem, anywhere,
+            vmem, vmem, vmem, anywhere, anywhere, anywhere,
+        ],
+        out_specs=vmem,
+        scratch_shapes=[
+            pltpu.VMEM(kv_cache.shape, bf16),
+            pltpu.VMEM(out_proj.shape, bf16),
+            pltpu.VMEM((cols, features, chunk), bf16),
+            pltpu.VMEM((cols, features, chunk), bf16),
+            pltpu.VMEM((cols, chunk, features), bf16),
+            pltpu.VMEM((states, HEAD_DIM), f32),
+            pltpu.VMEM((states, HEAD_DIM), f32),
+            pltpu.VMEM((states, HEAD_DIM), f32),
+            pltpu.VMEM((states, HEAD_DIM), bf16),
+            pltpu.VMEM((8, 128), f32),
+            pltpu.VMEM((peers, states, HEAD_DIM), bf16),
+            pltpu.VMEM((peers, 8, 128), f32),
+            pltpu.VMEM((states, HEAD_DIM), f32),
+            pltpu.VMEM((groups, rows, features), f32),
+            pltpu.VMEM((row_count, 128), f32),
+            pltpu.VMEM((peers, row_count, 128), f32),
+            pltpu.VMEM((peers, 2 * row_count, chunk), bf16),
+            pltpu.VMEM((peers, 2 * row_count, chunk), bf16),
+            pltpu.VMEM((row_count, chunk), bf16),
+            pltpu.VMEM((peers, row_count, chunk), bf16),
+            pltpu.VMEM((groups, rows, features), f32),
+            pltpu.VMEM((pools * groups, rows, features), f32),
+            dma((2,)),
+            dma((3, cols)),
+            dma((peers,)), dma((peers,)),
+            dma((peers,)), dma((peers,)),
+            dma((groups - 1,)), dma((groups - 1,)),
+            dma((peers,)), dma((peers,)),
+            dma((peers,)), dma((peers,)),
+            dma((peers,)), dma((peers,)),
+            dma((row_peers,)), dma((row_peers,)),
+        ],
+        compiler_params=pltpu.CompilerParams(
+            collective_id=0, has_side_effects=True, vmem_limit_bytes=48 * 2**20
+        ),
+    )(
+        queries,
+        fresh_kv,
+        kv_cache,
+        lengths,
+        residual,
+        out_proj,
+        norm_gain.reshape(1, -1),
+        router.T,
+        routes.T,
+        w_gate,
+        w_up,
+        w_down,
+    )
+
+
+def fits_kernel(mesh, w_gate, residual):
+    sizes = dict(mesh.shape)
+    chunk, left = divmod(w_gate.shape[1], sizes["grp"] * sizes["pool"] * sizes["col"])
+    states = residual.shape[0] // sizes["grp"] * HEADS
+    return (
+        left == 0
+        and chunk % 128 == 0
+        and residual.shape[0] % 16 == 0
+        and residual.shape[0] <= 128
+        and states <= 128
+        and sizes["grp"] % EXPERTS == 0
+    )
+
 
 def solution(mesh):
     placed = (
@@ -247,6 +697,11 @@
         P("col", "grp"),
         P("grp", "col"),
     )
-    return jax.shard_map(
-        local, mesh=mesh, in_specs=placed, out_specs=P("grp", "col"), check_vma=False
-    )
+
+    def whole(*args):
+        body = fused_local if fits_kernel(mesh, args[9], args[4]) else local
+        return jax.shard_map(
+            body, mesh=mesh, in_specs=placed, out_specs=P("grp", "col"), check_vma=False
+        )(*args)
+
+    return whole

time: 149 us -> 40.8 us (0.27)
  blocking collectives: 63.8 us -> 0 us
  waiting for transfers between devices: 50.5 us -> 0 us
  Pallas kernels: 0 us -> 31.6 us
  between operations: 13.5 us -> 0.02 us
  other arithmetic: 5.68 us -> 0 us
  matrix products: 4.52 us -> 0 us
  starting transfers between devices: 3.39 us -> 0 us
  local copies, waits for them, and re-layouts: 6.32 us -> 8.65 us
    psum x1 -> x0, waiting for transfers between devices: 47 us -> none  [local(): gate_sum, up_sum, squares, logit_sum = lax.psum(partials, 'col')]
    all_gather x3 -> x0, blocking collectives: 38.8 us -> none  [merged(): gathered = jax.tree.map(lambda a: lax.all_gather(a, axis), part)]
    pallas_call x0 -> x1, Pallas kernels: none -> 31.6 us  [fused_local(): pl.pallas_call(fused_kernel, out_shape=jax.ShapeDtypeStruct((rows, featur...]
    all_to_all x1 -> x0, blocking collectives: 15.8 us -> none  [local(): lax.all_to_all(outgoing_back, ('pool', 'grp'), split_axis=0, concat_axis=...]
    psum x1 -> x0, blocking collectives: 9.24 us -> none  [local(): gate_sum, up_sum, squares, logit_sum = lax.psum(partials, 'col')]
    unnamed x6 -> x19, local copies, waits for them, and re-layouts: 1.73 us -> 8.65 us
    dot_general x8 -> x0, matrix products: 4.52 us -> none  [the longest x1 2.84 us: local(): projected = jnp.dot(attended, out_proj, preferred_element_type=jnp.float32)]
    all_to_all x1 -> x0, waiting for transfers between devices: 3.49 us -> none  [local(): lax.all_to_all(outgoing, ('pool', 'grp'), split_axis=0, concat_axis=0, ti...]
  transfers between devices with their start and end apart: 2 -> 0, of which waited for: 2 -> 0; matrix products, arithmetic and copies ran while one was open for 1% -> 0% of each run, Pallas kernels for 0% -> 0%
where the time goes in v1:
time: 40.8 us; the launch traced here: 40.3 us
  Pallas kernels  31.6 us (77%)
  local copies, waits for them, and re-layouts  8.65 us (21%)
    pallas_call x1, Pallas kernels, fused_local(): pl.pallas_call(fused_kernel, out_shape=jax.ShapeDtypeStruct((rows, featur...  31.6 us
    unnamed x19, local copies, waits for them, and re-layouts  8.65 us

profile of v1, /device:TPU:0, one launch (start us, length us, event | category | flops | bytes accessed | tf_op | source)
XLA Modules:
  0.0 40.3 jit_solution(14963863393029056656)
XLA Ops:
  0.0 0.0 copy-start
  0.0 2.2 %copy-done = bf16[2048,1024]{1,0:T(8,128)(2,1)S(1)} copy-done((bf16[2048,1024]{1,0:T(8,128)(2,1)S(1)}, bf16[2048,1024]{1,0:T(8,128)(2,1)}, u32[]{:S(2)}) %copy-start) | copy-done | bytes 4194328
  2.2 0.0 copy-start.1
  2.2 1.0 %copy-done.1 = bf16[4,64,1024]{2,1,0:T(8,128)(2,1)S(1)} copy-done((bf16[4,64,1024]{2,1,0:T(8,128)(2,1)S(1)}, bf16[4,64,1024]{2,1,0:T(8,128)(2,1)}, u32[]{:S(2)}) %copy-start.1) | copy-done | bytes 524312
  3.2 0.0 copy-start.2
  3.2 0.7 %copy-done.2 = bf16[4,2048]{1,0:T(4,128)(2,1)S(1)} copy-done((bf16[4,2048]{1,0:T(4,128)(2,1)S(1)}, bf16[4,2048]{1,0:T(4,128)(2,1)}, u32[]{:S(2)}) %copy-start.2) | copy-done | bytes 16408
  3.9 0.0 copy-start.3
  4.0 0.7 %copy-done.3 = bf16[4,1024]{1,0:T(4,128)(2,1)S(1)} copy-done((bf16[4,1024]{1,0:T(4,128)(2,1)S(1)}, bf16[4,1024]{1,0:T(4,128)(2,1)}, u32[]{:S(2)}) %copy-start.3) | copy-done | bytes 8216
  4.6 0.0 copy-start.4
  4.6 0.7 %copy-done.4 = bf16[4,1024]{1,0:T(4,128)(2,1)S(1)} copy-done((bf16[4,1024]{1,0:T(4,128)(2,1)S(1)}, bf16[4,1024]{1,0:T(4,128)(2,1)}, u32[]{:S(2)}) %copy-start.4) | copy-done | bytes 8216
  5.3 0.0 copy-start.5
  5.3 0.7 %copy-done.5 = bf16[1024,4]{0,1:T(4,128)(2,1)S(1)} copy-done((bf16[1024,4]{0,1:T(4,128)(2,1)S(1)}, bf16[1024,4]{0,1:T(4,128)(2,1)}, u32[]{:S(2)}) %copy-start.5) | copy-done | bytes 8216
  6.0 0.0 copy-start.6
  6.0 0.7 %copy-done.6 = f32[1024]{0:T(1024)S(1)} copy-done((f32[1024]{0:T(1024)S(1)}, f32[1024]{0:T(1024)}, u32[]{:S(2)}) %copy-start.6) | copy-done | bytes 4120
  6.7 0.0 copy-start.7
  6.7 0.7 %copy-done.7 = s32[16,2]{0,1:T(2,128)S(1)} copy-done((s32[16,2]{0,1:T(2,128)S(1)}, s32[16,2]{0,1:T(2,128)}, u32[]{:S(2)}) %copy-start.7) | copy-done | bytes 152
  7.4 0.0 copy-start.8
  7.4 0.7 %copy-done.8 = s32[4]{0:T(128)S(1)} copy-done((s32[4]{0:T(128)S(1)}, s32[4]{0:T(128)}, u32[]{:S(2)}) %copy-start.8) | copy-done | bytes 40
  8.1 31.6 %shard_map.118 = bf16[4,1024]{1,0:T(4,128)(2,1)S(1)} custom-call(bf16[4,2048]{1,0:T(4,128)(2,1)S(1)} %copy-done.2, bf16[4,1024]{1,0:T(4,128)(2,1)S(1)} %copy-done.3, bf16[4,64,1024]{2,1,0:T(8,128)(2,1)S(1)} %copy-done.1, s32[4]{0:T(128)S(1)} %copy-done.8, bf16[4,1024]{1,0:T(4,128)(2,1)S(1)} %copy-done.4, bf16[2048,1024]{1,0:T(8,128)(2,1)S(1)} %copy-done, ...), custom_call_target="tpu_custom_call" | custom-call | tf_op jit(solution)/shard_map/pallas_call | solution.py:611
  39.7 0.6 %copy.14 = bf16[4,1024]{1,0:T(4,128)(2,1)} copy(bf16[4,1024]{1,0:T(4,128)(2,1)S(1)} %shard_map.118) | data formatting | bytes 16384
Async XLA Ops:
  0.0 2.2 %copy-start = (bf16[2048,1024]{1,0:T(8,128)(2,1)S(1)}, bf16[2048,1024]{1,0:T(8,128)(2,1)}, u32[]{:S(2)}) copy-start(bf16[2048,1024]{1,0:T(8,128)(2,1)} %proj_hbm.1) | copy-start | bytes 12582916
  2.2 1.0 %copy-start.1 = (bf16[4,64,1024]{2,1,0:T(8,128)(2,1)S(1)}, bf16[4,64,1024]{2,1,0:T(8,128)(2,1)}, u32[]{:S(2)}) copy-start(bf16[4,64,1024]{2,1,0:T(8,128)(2,1)} %kv_hbm.1) | copy-start | bytes 1572868
  3.2 0.7 %copy-start.2 = (bf16[4,2048]{1,0:T(4,128)(2,1)S(1)}, bf16[4,2048]{1,0:T(4,128)(2,1)}, u32[]{:S(2)}) copy-start(bf16[4,2048]{1,0:T(4,128)(2,1)} %queries.1) | copy-start | bytes 49156
  3.9 0.7 %copy-start.3 = (bf16[4,1024]{1,0:T(4,128)(2,1)S(1)}, bf16[4,1024]{1,0:T(4,128)(2,1)}, u32[]{:S(2)}) copy-start(bf16[4,1024]{1,0:T(4,128)(2,1)} %fresh.1) | copy-start | bytes 24580
  4.6 0.7 %copy-start.4 = (bf16[4,1024]{1,0:T(4,128)(2,1)S(1)}, bf16[4,1024]{1,0:T(4,128)(2,1)}, u32[]{:S(2)}) copy-start(bf16[4,1024]{1,0:T(4,128)(2,1)} %residual.1) | copy-start | bytes 24580
  5.3 0.7 %copy-start.5 = (bf16[1024,4]{0,1:T(4,128)(2,1)S(1)}, bf16[1024,4]{0,1:T(4,128)(2,1)}, u32[]{:S(2)}) copy-start(bf16[1024,4]{0,1:T(4,128)(2,1)} %param.19) | copy-start | bytes 24580
  6.0 0.7 %copy-start.6 = (f32[1024]{0:T(1024)S(1)}, f32[1024]{0:T(1024)}, u32[]{:S(2)}) copy-start(f32[1024]{0:T(1024)} %param.18) | copy-start | bytes 12292
  6.7 0.7 %copy-start.7 = (s32[16,2]{0,1:T(2,128)S(1)}, s32[16,2]{0,1:T(2,128)}, u32[]{:S(2)}) copy-start(s32[16,2]{0,1:T(2,128)} %param.20) | copy-start | bytes 388
  7.4 0.7 %copy-start.8 = (s32[4]{0:T(128)S(1)}, s32[4]{0:T(128)}, u32[]{:S(2)}) copy-start(s32[4]{0:T(128)} %lengths.1) | copy-start | bytes 52

commit v2 on v1

--- a/solution.py
+++ b/solution.py
@@ -237,19 +237,26 @@
 
 
 def fused_kernel(
-    queries,
-    fresh,
+    queries_hbm,
+    fresh_hbm,
     kv_hbm,
-    lengths,
-    residual,
+    lengths_hbm,
+    residual_hbm,
     proj_hbm,
-    gain,
-    router,
-    routes,
+    gain_hbm,
+    router_hbm,
+    routes_hbm,
     gate_hbm,
     up_hbm,
     down_hbm,
     out,
+    queries,
+    fresh,
+    lengths,
+    residual,
+    gain,
+    router,
+    routes,
     kv,
     proj,
     gate_w,
@@ -303,9 +310,32 @@
     states = rows * HEADS
     first_column = pool * (chunk * cols)
 
+    def col_peer(k):
+        return (pool, grp, lax.rem(col + k, cols))
+
+    def row_peer(kp, kg):
+        return (lax.rem(pool + kp, pools), lax.rem(grp + kg, groups), col)
+
+    row_steps = [(kp, kg) for kg in range(groups) for kp in range(pools) if kp or kg]
+    barrier = pltpu.get_barrier_semaphore()
+    for k in range(1, cols):
+        pl.semaphore_signal(barrier, inc=1, device_id=col_peer(k), device_id_type=MESH)
+    for kp, kg in row_steps:
+        pl.semaphore_signal(barrier, inc=1, device_id=row_peer(kp, kg), device_id_type=MESH)
+
+    operands = (
+        (queries_hbm, queries),
+        (fresh_hbm, fresh),
+        (lengths_hbm, lengths),
+        (kv_hbm, kv),
+        (residual_hbm, residual),
+        (gain_hbm, gain),
+        (router_hbm, router),
+        (routes_hbm, routes),
+        (proj_hbm, proj),
+    )
     loads = [
-        pltpu.make_async_copy(kv_hbm, kv, load_sem.at[0]),
-        pltpu.make_async_copy(proj_hbm, proj, load_sem.at[1]),
+        pltpu.make_async_copy(src, dst, load_sem.at[i]) for i, (src, dst) in enumerate(operands)
     ]
     for load in loads:
         load.start()
@@ -328,19 +358,8 @@
         )
         down_loads[k].start()
 
-    def col_peer(k):
-        return (pool, grp, lax.rem(col + k, cols))
-
-    def row_peer(kp, kg):
-        return (lax.rem(pool + kp, pools), lax.rem(grp + kg, groups), col)
-
-    row_steps = [(kp, kg) for kg in range(groups) for kp in range(pools) if kp or kg]
-    barrier = pltpu.get_barrier_semaphore()
-    for k in range(1, cols):
-        pl.semaphore_signal(barrier, inc=1, device_id=col_peer(k), device_id_type=MESH)
-    for kp, kg in row_steps:
-        pl.semaphore_signal(barrier, inc=1, device_id=row_peer(kp, kg), device_id_type=MESH)
-
+    loads[0].wait()
+    loads[1].wait()
     wide_queries = queries[...].astype(jnp.float32)
     wide_fresh = fresh[...].astype(jnp.float32)
     for h in range(HEADS):
@@ -355,7 +374,8 @@
     own_score = jnp.sum(query_rows[...] * key_rows[...], axis=1, keepdims=True) * scale
     head_of = lax.broadcasted_iota(jnp.int32, (HEADS, HEAD_DIM), 0) // group_size
     place = col * positions + lax.broadcasted_iota(jnp.int32, (HEADS, positions), 1)
-    loads[0].wait()
+    loads[2].wait()
+    loads[3].wait()
     peaks, totals = [], []
     for r in range(rows):
         head_rows = query_rows[r * HEADS : (r + 1) * HEADS, :]
@@ -417,7 +437,7 @@
             copy.start()
             state_copies.append(copy)
     for copy in state_copies:
-        copy.wait()
+        copy.wait_recv()
 
     all_peaks, all_totals = [peak], [total]
     for k in range(1, cols):
@@ -442,10 +462,22 @@
     attended = jnp.concatenate(
         [attended_rows[pl.ds(h, rows, stride=HEADS), :] for h in range(HEADS)], axis=1
     ).astype(jnp.bfloat16)
-    loads[1].wait()
+    for load in loads[4:]:
+        load.wait()
     projected = jnp.dot(attended, proj[...], preferred_element_type=jnp.float32)
     stream = (residual[...].astype(jnp.float32) + projected).astype(jnp.bfloat16)
-    streams[grp] = stream.astype(jnp.float32)
+    pack = streams.shape[1] // rows
+    packed_width = streams.shape[2]
+
+    def packed_rows(block):
+        return jnp.concatenate(
+            [block[:, i * packed_width : (i + 1) * packed_width] for i in range(pack)], axis=0
+        ).astype(jnp.bfloat16)
+
+    def unpacked_rows(block):
+        return jnp.concatenate([block[i * rows : (i + 1) * rows, :] for i in range(pack)], axis=1)
+
+    streams[grp] = packed_rows(stream.astype(jnp.float32))
 
     stream_copies = []
     for kg in range(1, groups):
@@ -460,9 +492,9 @@
         copy.start()
         stream_copies.append(copy)
     for copy in stream_copies:
-        copy.wait()
-
-    wide = jnp.concatenate([streams[g] for g in range(groups)], axis=0)
+        copy.wait_recv()
+
+    wide = jnp.concatenate([unpacked_rows(streams[g].astype(jnp.float32)) for g in range(groups)], axis=0)
     scaled = (wide * gain[...]).astype(jnp.bfloat16)
     squares = jnp.sum(wide * wide, axis=1, keepdims=True)
     logit_part = lax.dot_general(
@@ -507,7 +539,7 @@
         part_copies.append(copy)
 
     for copy in part_copies[: cols - 1]:
-        copy.wait()
+        copy.wait_recv()
     sums = sums_own[...]
     for k in range(1, cols):
         sums = sums + sums_in[k - 1]
@@ -531,9 +563,8 @@
         rival_logit = rival_logit + jnp.where(rival == float(j), logit, 0.0)
     row_weight = jnp.where(chosen, 1.0 / (1.0 + jnp.exp(rival_logit - own_logit)), 0.0)
 
-    for copy in part_copies[cols - 1 :]:
-        copy.wait()
     for k in range(1, cols):
+        part_copies[cols - 2 + k].wait_recv()
         gate_part = gate_part + part_in[k - 1, :row_count, :].astype(jnp.float32)
         up_part = up_part + part_in[k - 1, row_count:, :].astype(jnp.float32)
     gate = gate_part * inverse
@@ -555,11 +586,11 @@
     down_loads[0].wait()
     result = jnp.dot(hidden, down_w[0], preferred_element_type=jnp.float32)
     for k in range(1, cols):
-        hidden_copies[k - 1].wait()
+        hidden_copies[k - 1].wait_recv()
         down_loads[k].wait()
         result = result + jnp.dot(hidden_in[k - 1], down_w[k], preferred_element_type=jnp.float32)
     for g in range(groups):
-        pieces[g] = result[g * rows : (g + 1) * rows, :]
+        pieces[g] = packed_rows(result[g * rows : (g + 1) * rows, :])
     me = pool * groups + grp
     returned[me] = pieces[grp]
     piece_copies = []
@@ -576,11 +607,13 @@
         copy.start()
         piece_copies.append(copy)
     for copy in piece_copies:
-        copy.wait()
-    final = stream.astype(jnp.float32)
+        copy.wait_recv()
+    final = streams[grp].astype(jnp.float32)
     for i in range(pools * groups):
-        final = final + returned[i]
-    out[...] = final.astype(jnp.bfloat16)
+        final = final + returned[i].astype(jnp.float32)
+    out[...] = unpacked_rows(final).astype(jnp.bfloat16)
+    for copy in state_copies + stream_copies + part_copies + hidden_copies + piece_copies:
+        copy.wait_send()
 
 
 def fused_local(
@@ -603,20 +636,23 @@
     chunk = w_gate.shape[1] // (pools * cols)
     states = rows * HEADS
     f32, bf16 = jnp.float32, jnp.bfloat16
-    vmem, anywhere = pl.BlockSpec(memory_space=pltpu.VMEM), pl.BlockSpec(memory_space=pl.ANY)
-    scalars = pl.BlockSpec(memory_space=pltpu.SMEM)
+    packed_shape = (rows * (16 // rows), features // (16 // rows))
     peers = cols - 1
     row_peers = pools * groups - 1
     dma = pltpu.SemaphoreType.DMA
     return pl.pallas_call(
         fused_kernel,
         out_shape=jax.ShapeDtypeStruct((rows, features), bf16),
-        in_specs=[
-            vmem, vmem, anywhere, scalars, vmem, anywhere,
-            vmem, vmem, vmem, anywhere, anywhere, anywhere,
-        ],
-        out_specs=vmem,
+        in_specs=[pl.BlockSpec(memory_space=pl.ANY)] * 12,
+        out_specs=pl.BlockSpec(memory_space=pltpu.VMEM),
         scratch_shapes=[
+            pltpu.VMEM(queries.shape, bf16),
+            pltpu.VMEM(fresh_kv.shape, bf16),
+            pltpu.SMEM(lengths.shape, jnp.int32),
+            pltpu.VMEM(residual.shape, bf16),
+            pltpu.VMEM((1, features), f32),
+            pltpu.VMEM((EXPERTS, features), bf16),
+            pltpu.VMEM(routes.shape[::-1], jnp.int32),
             pltpu.VMEM(kv_cache.shape, bf16),
             pltpu.VMEM(out_proj.shape, bf16),
             pltpu.VMEM((cols, features, chunk), bf16),
@@ -630,16 +666,16 @@
             pltpu.VMEM((peers, states, HEAD_DIM), bf16),
             pltpu.VMEM((peers, 8, 128), f32),
             pltpu.VMEM((states, HEAD_DIM), f32),
-            pltpu.VMEM((groups, rows, features), f32),
+            pltpu.VMEM((groups,) + packed_shape, bf16),
             pltpu.VMEM((row_count, 128), f32),
             pltpu.VMEM((peers, row_count, 128), f32),
             pltpu.VMEM((peers, 2 * row_count, chunk), bf16),
             pltpu.VMEM((peers, 2 * row_count, chunk), bf16),
             pltpu.VMEM((row_count, chunk), bf16),
             pltpu.VMEM((peers, row_count, chunk), bf16),
-            pltpu.VMEM((groups, rows, features), f32),
-            pltpu.VMEM((pools * groups, rows, features), f32),
-            dma((2,)),
+            pltpu.VMEM((groups,) + packed_shape, bf16),
+            pltpu.VMEM((pools * groups,) + packed_shape, bf16),
+            dma((9,)),
             dma((3, cols)),
             dma((peers,)), dma((peers,)),
             dma((peers,)), dma((peers,)),
@@ -650,7 +686,7 @@
             dma((row_peers,)), dma((row_peers,)),
         ],
         compiler_params=pltpu.CompilerParams(
-            collective_id=0, has_side_effects=True, vmem_limit_bytes=48 * 2**20
+            collective_id=0, has_side_effects=True, vmem_limit_bytes=62 * 2**20
         ),
     )(
         queries,
@@ -671,11 +707,14 @@
 def fits_kernel(mesh, w_gate, residual):
     sizes = dict(mesh.shape)
     chunk, left = divmod(w_gate.shape[1], sizes["grp"] * sizes["pool"] * sizes["col"])
-    states = residual.shape[0] // sizes["grp"] * HEADS
+    rows = residual.shape[0] // sizes["grp"]
+    states = rows * HEADS
     return (
         left == 0
         and chunk % 128 == 0
         and residual.shape[0] % 16 == 0
+        and 16 % rows == 0
+        and residual.shape[1] // sizes["col"] % (16 // rows * 128) == 0
         and residual.shape[0] <= 128
         and states <= 128
         and sizes["grp"] % EXPERTS == 0

time: 40.8 us -> 35.2 us (0.86)
  local copies, waits for them, and re-layouts: 8.65 us -> 1.3 us
  Pallas kernels: 31.6 us -> 33.7 us
    unnamed x19 -> x1, local copies, waits for them, and re-layouts: 8.65 us -> 1.3 us
    pallas_call x1, Pallas kernels: 31.6 us -> 33.7 us  [fused_local(): pl.pallas_call(fused_kernel, out_shape=jax.ShapeDtypeStruct((rows, featur...]
where the time goes in v2:
time: 35.2 us; the launch traced here: 35 us
  Pallas kernels  33.7 us (96%)
  local copies, waits for them, and re-layouts  1.3 us (4%)
    pallas_call x1, Pallas kernels, fused_local(): pl.pallas_call(fused_kernel, out_shape=jax.ShapeDtypeStruct((rows, featur...  33.7 us
    unnamed x1, local copies, waits for them, and re-layouts  1.3 us

profile of v2, /device:TPU:0, one launch (start us, length us, event | category | flops | bytes accessed | tf_op | source)
XLA Modules:
  0.0 35.0 jit_solution(2399934086111275509)
XLA Ops:
  0.0 33.7 %shard_map.118 = bf16[4,1024]{1,0:T(4,128)(2,1)} custom-call(bf16[4,2048]{1,0:T(4,128)(2,1)} %queries_hbm.1, bf16[4,1024]{1,0:T(4,128)(2,1)} %fresh_hbm.1, bf16[4,64,1024]{2,1,0:T(8,128)(2,1)} %kv_hbm.1, s32[4]{0:T(128)} %lengths_hbm.1, bf16[4,1024]{1,0:T(4,128)(2,1)} %residual_hbm.1, bf16[2048,1024]{1,0:T(8,128)(2,1)} %proj_hbm.1, f32[1,1024]{1,0:T(1,128)} %bitcast.4, ...), custom_call_target="tpu_custom_call" | custom-call | tf_op jit(solution)/shard_map/pallas_call | solution.py:643
  33.7 1.3 %copy.14 = bf16[4,1024]{1,0:T(4,128)(2,1)} copy(bf16[4,1024]{1,0:T(4,128)(2,1)} %shard_map.118) | data formatting | bytes 16384

commit v3 on v2

--- a/solution.py
+++ b/solution.py
@@ -348,15 +348,14 @@
             gate_hbm.at[:, window], gate_w.at[k], weight_sem.at[0, k]
         )
         up_loads[k] = pltpu.make_async_copy(up_hbm.at[:, window], up_w.at[k], weight_sem.at[1, k])
-        gate_loads[k].start()
-        up_loads[k].start()
+        gate_loads[k].start(priority=1)
+        up_loads[k].start(priority=1)
     for k in range(cols):
         source = lax.rem(col + cols - k, cols)
         window = pl.ds(pl.multiple_of(first_column + source * chunk, 128), chunk)
         down_loads[k] = pltpu.make_async_copy(
             down_hbm.at[window, :], down_w.at[k], weight_sem.at[2, k]
         )
-        down_loads[k].start()
 
     loads[0].wait()
     loads[1].wait()
@@ -538,6 +537,8 @@
         copy.start()
         part_copies.append(copy)
 
+    for k in range(cols):
+        down_loads[k].start()
     for copy in part_copies[: cols - 1]:
         copy.wait_recv()
     sums = sums_own[...]

time: 35.2 us -> 32.1 us (0.912)
  Pallas kernels: 33.7 us -> 30.5 us
    pallas_call x1, Pallas kernels: 33.7 us -> 30.5 us  [fused_local(): pl.pallas_call(fused_kernel, out_shape=jax.ShapeDtypeStruct((rows, featur...]
where the time goes in v3:
time: 32.1 us; the launch traced here: 31.8 us
  Pallas kernels  30.5 us (95%)
  local copies, waits for them, and re-layouts  1.3 us (4%)
    pallas_call x1, Pallas kernels, fused_local(): pl.pallas_call(fused_kernel, out_shape=jax.ShapeDtypeStruct((rows, featur...  30.5 us
    unnamed x1, local copies, waits for them, and re-layouts  1.3 us

profile of v3, /device:TPU:0, one launch (start us, length us, event | category | flops | bytes accessed | tf_op | source)
XLA Modules:
  0.0 31.8 jit_solution(8713175978393932959)
XLA Ops:
  0.0 30.5 %shard_map.118 = bf16[4,1024]{1,0:T(4,128)(2,1)} custom-call(bf16[4,2048]{1,0:T(4,128)(2,1)} %queries_hbm.1, bf16[4,1024]{1,0:T(4,128)(2,1)} %fresh_hbm.1, bf16[4,64,1024]{2,1,0:T(8,128)(2,1)} %kv_hbm.1, s32[4]{0:T(128)} %lengths_hbm.1, bf16[4,1024]{1,0:T(4,128)(2,1)} %residual_hbm.1, bf16[2048,1024]{1,0:T(8,128)(2,1)} %proj_hbm.1, f32[1,1024]{1,0:T(1,128)} %bitcast.4, ...), custom_call_target="tpu_custom_call" | custom-call | tf_op jit(solution)/shard_map/pallas_call | solution.py:644
  30.5 1.3 %copy.14 = bf16[4,1024]{1,0:T(4,128)(2,1)} copy(bf16[4,1024]{1,0:T(4,128)(2,1)} %shard_map.118) | data formatting | bytes 16384

commit v4 on v3

--- a/solution.py
+++ b/solution.py
@@ -490,10 +490,33 @@
         )
         copy.start()
         stream_copies.append(copy)
+    row_count = rows * groups
+    slots = CAPB * groups
+    expert_label = (grp // (groups // EXPERTS)).astype(jnp.float32)
+    square = (row_count, row_count)
+    down_index = lax.broadcasted_iota(jnp.int32, square, 0)
+    across_index = lax.broadcasted_iota(jnp.int32, square, 1)
+    named = routes[...].astype(jnp.float32)
+    first, second = named[0:1, :], named[1:2, :]
+    hit_row = jnp.where(first == expert_label, 1.0, 0.0) + jnp.where(
+        second == expert_label, 1.0, 0.0
+    )
+    hit_col = jnp.sum(jnp.where(down_index == across_index, hit_row, 0.0), axis=1, keepdims=True)
+    rank_row = jnp.sum(jnp.where(down_index < across_index, hit_col, 0.0), axis=0, keepdims=True)
+    rank_col = jnp.sum(jnp.where(across_index < down_index, hit_row, 0.0), axis=1, keepdims=True)
+    to_slots = jnp.where(down_index.astype(jnp.float32) == rank_row, hit_row, 0.0)
+    to_rows = jnp.where(across_index.astype(jnp.float32) == rank_col, hit_col, 0.0)
+    filled = jnp.sum(to_slots, axis=1, keepdims=True) > 0.5
+    rival = jnp.sum(to_slots * (first + second - expert_label), axis=1, keepdims=True)
     for copy in stream_copies:
         copy.wait_recv()
 
     wide = jnp.concatenate([unpacked_rows(streams[g].astype(jnp.float32)) for g in range(groups)], axis=0)
+    wide = jnp.dot(
+        to_slots.astype(jnp.bfloat16),
+        wide.astype(jnp.bfloat16),
+        preferred_element_type=jnp.float32,
+    )
     scaled = (wide * gain[...]).astype(jnp.bfloat16)
     squares = jnp.sum(wide * wide, axis=1, keepdims=True)
     logit_part = lax.dot_general(
@@ -516,7 +539,20 @@
         )
         copy.start()
         part_copies.append(copy)
-    row_count = rows * groups
+    side = part_send.shape[2] - chunk
+    extra = slots - 8
+
+    def packed_parts(gate, up):
+        rest = jnp.concatenate([gate[8:slots, :], up[8:slots, :]], axis=0)
+        rest = jnp.concatenate([rest, jnp.zeros((8, 2 * side - chunk), jnp.float32)], axis=1)
+        return jnp.concatenate(
+            [
+                jnp.concatenate([gate[:8, :], rest[:, :side]], axis=1),
+                jnp.concatenate([up[:8, :], rest[:, side:]], axis=1),
+            ],
+            axis=0,
+        )
+
     for k in steps:
         gate_loads[k].wait()
         gate_part = jnp.dot(scaled, gate_w[k], preferred_element_type=jnp.float32)
@@ -524,8 +560,7 @@
         up_part = jnp.dot(scaled, up_w[k], preferred_element_type=jnp.float32)
         if k == 0:
             break
-        part_send[k - 1, :row_count, :] = gate_part.astype(jnp.bfloat16)
-        part_send[k - 1, row_count:, :] = up_part.astype(jnp.bfloat16)
+        part_send[k - 1] = packed_parts(gate_part, up_part).astype(jnp.bfloat16)
         copy = pltpu.make_async_remote_copy(
             src_ref=part_send.at[k - 1],
             dst_ref=part_in.at[k - 1],
@@ -541,33 +576,26 @@
         down_loads[k].start()
     for copy in part_copies[: cols - 1]:
         copy.wait_recv()
+    total_part = packed_parts(gate_part, up_part)
     sums = sums_own[...]
     for k in range(1, cols):
         sums = sums + sums_in[k - 1]
     inverse = lax.rsqrt(sums[:, EXPERTS : EXPERTS + 1] / D + EPSILON)
-    expert = grp // (groups // EXPERTS)
-    square = (row_count, row_count)
-    row_diagonal = lax.broadcasted_iota(jnp.int32, square, 0) == lax.broadcasted_iota(
-        jnp.int32, square, 1
-    )
-    named = routes[...].astype(jnp.float32)
-    first = jnp.sum(jnp.where(row_diagonal, named[0:1, :], 0.0), axis=1, keepdims=True)
-    second = jnp.sum(jnp.where(row_diagonal, named[1:2, :], 0.0), axis=1, keepdims=True)
-    expert_label = expert.astype(jnp.float32)
-    chosen = jnp.logical_or(first == expert_label, second == expert_label)
-    rival = first + second - expert_label
     own_logit = jnp.zeros_like(inverse)
     rival_logit = jnp.zeros_like(inverse)
     for j in range(EXPERTS):
         logit = sums[:, j : j + 1] * inverse
         own_logit = own_logit + jnp.where(expert_label == float(j), logit, 0.0)
         rival_logit = rival_logit + jnp.where(rival == float(j), logit, 0.0)
-    row_weight = jnp.where(chosen, 1.0 / (1.0 + jnp.exp(rival_logit - own_logit)), 0.0)
+    row_weight = jnp.where(filled, 1.0 / (1.0 + jnp.exp(rival_logit - own_logit)), 0.0)
 
     for k in range(1, cols):
         part_copies[cols - 2 + k].wait_recv()
-        gate_part = gate_part + part_in[k - 1, :row_count, :].astype(jnp.float32)
-        up_part = up_part + part_in[k - 1, row_count:, :].astype(jnp.float32)
+        total_part = total_part + part_in[k - 1].astype(jnp.float32)
+    rest = jnp.concatenate([total_part[:8, chunk:], total_part[8:, chunk:]], axis=1)[:, :chunk]
+    blank = jnp.zeros((row_count - slots, chunk), jnp.float32)
+    gate_part = jnp.concatenate([total_part[:8, :chunk], rest[:extra, :], blank], axis=0)
+    up_part = jnp.concatenate([total_part[8:, :chunk], rest[extra:, :], blank], axis=0)
     gate = gate_part * inverse
     up = up_part * inverse
     hidden = (gate / (1.0 + jnp.exp(-gate)) * up * row_weight).astype(jnp.bfloat16)
@@ -590,6 +618,11 @@
         hidden_copies[k - 1].wait_recv()
         down_loads[k].wait()
         result = result + jnp.dot(hidden_in[k - 1], down_w[k], preferred_element_type=jnp.float32)
+    result = jnp.dot(
+        to_rows.astype(jnp.bfloat16),
+        result.astype(jnp.bfloat16),
+        preferred_element_type=jnp.float32,
+    )
     for g in range(groups):
         pieces[g] = packed_rows(result[g * rows : (g + 1) * rows, :])
     me = pool * groups + grp
@@ -670,8 +703,8 @@
             pltpu.VMEM((groups,) + packed_shape, bf16),
             pltpu.VMEM((row_count, 128), f32),
             pltpu.VMEM((peers, row_count, 128), f32),
-            pltpu.VMEM((peers, 2 * row_count, chunk), bf16),
-            pltpu.VMEM((peers, 2 * row_count, chunk), bf16),
+            pltpu.VMEM((peers, 16, chunk + (chunk + 255) // 256 * 128), bf16),
+            pltpu.VMEM((peers, 16, chunk + (chunk + 255) // 256 * 128), bf16),
             pltpu.VMEM((row_count, chunk), bf16),
             pltpu.VMEM((peers, row_count, chunk), bf16),
             pltpu.VMEM((groups,) + packed_shape, bf16),
@@ -713,10 +746,10 @@
     return (
         left == 0
         and chunk % 128 == 0
-        and residual.shape[0] % 16 == 0
+        and residual.shape[0] == 16
+        and CAPB * sizes["grp"] == 12
         and 16 % rows == 0
         and residual.shape[1] // sizes["col"] % (16 // rows * 128) == 0
-        and residual.shape[0] <= 128
         and states <= 128
         and sizes["grp"] % EXPERTS == 0
     )

time: 32.1 us -> 31.3 us (0.975)
  Pallas kernels: 30.5 us -> 29.7 us
    pallas_call x1, Pallas kernels: 30.5 us -> 29.7 us  [fused_local(): pl.pallas_call(fused_kernel, out_shape=jax.ShapeDtypeStruct((rows, featur...]
where the time goes in v4:
time: 31.3 us; the launch traced here: 31 us
  Pallas kernels  29.7 us (95%)
  local copies, waits for them, and re-layouts  1.3 us (4%)
    pallas_call x1, Pallas kernels, fused_local(): pl.pallas_call(fused_kernel, out_shape=jax.ShapeDtypeStruct((rows, featur...  29.7 us
    unnamed x1, local copies, waits for them, and re-layouts  1.3 us

profile of v4, /device:TPU:0, one launch (start us, length us, event | category | flops | bytes accessed | tf_op | source)
XLA Modules:
  0.0 31.0 jit_solution(7032489623509168271)
XLA Ops:
  0.0 29.7 %shard_map.118 = bf16[4,1024]{1,0:T(4,128)(2,1)} custom-call(bf16[4,2048]{1,0:T(4,128)(2,1)} %queries_hbm.1, bf16[4,1024]{1,0:T(4,128)(2,1)} %fresh_hbm.1, bf16[4,64,1024]{2,1,0:T(8,128)(2,1)} %kv_hbm.1, s32[4]{0:T(128)} %lengths_hbm.1, bf16[4,1024]{1,0:T(4,128)(2,1)} %residual_hbm.1, bf16[2048,1024]{1,0:T(8,128)(2,1)} %proj_hbm.1, f32[1,1024]{1,0:T(1,128)} %bitcast.4, ...), custom_call_target="tpu_custom_call" | custom-call | tf_op jit(solution)/shard_map/pallas_call | solution.py:677
  29.7 1.3 %copy.14 = bf16[4,1024]{1,0:T(4,128)(2,1)} copy(bf16[4,1024]{1,0:T(4,128)(2,1)} %shard_map.118) | data formatting | bytes 16384

commit v5 on v4

--- a/solution.py
+++ b/solution.py
@@ -339,7 +339,7 @@
     ]
     for load in loads:
         load.start()
-    steps = list(range(1, cols)) + [0]
+    steps = [cols // 2] + [k for k in range(1, cols) if k != cols // 2] + [0]
     gate_loads, up_loads, down_loads = {}, {}, {}
     for k in steps:
         owner = lax.rem(col + k, cols)
@@ -589,8 +589,8 @@
         rival_logit = rival_logit + jnp.where(rival == float(j), logit, 0.0)
     row_weight = jnp.where(filled, 1.0 / (1.0 + jnp.exp(rival_logit - own_logit)), 0.0)
 
-    for k in range(1, cols):
-        part_copies[cols - 2 + k].wait_recv()
+    for i, k in enumerate(steps[:-1]):
+        part_copies[cols - 1 + i].wait_recv()
         total_part = total_part + part_in[k - 1].astype(jnp.float32)
     rest = jnp.concatenate([total_part[:8, chunk:], total_part[8:, chunk:]], axis=1)[:, :chunk]
     blank = jnp.zeros((row_count - slots, chunk), jnp.float32)

time: 31.3 us -> 30.9 us (0.987)
  Pallas kernels: 29.7 us -> 29.3 us
    pallas_call x1, Pallas kernels: 29.7 us -> 29.3 us  [fused_local(): pl.pallas_call(fused_kernel, out_shape=jax.ShapeDtypeStruct((rows, featur...]
where the time goes in v5:
time: 30.9 us; the launch traced here: 30.6 us
  Pallas kernels  29.3 us (95%)
  local copies, waits for them, and re-layouts  1.3 us (4%)
    pallas_call x1, Pallas kernels, fused_local(): pl.pallas_call(fused_kernel, out_shape=jax.ShapeDtypeStruct((rows, featur...  29.3 us
    unnamed x1, local copies, waits for them, and re-layouts  1.3 us

profile of v5, /device:TPU:0, one launch (start us, length us, event | category | flops | bytes accessed | tf_op | source)
XLA Modules:
  0.0 30.6 jit_solution(2192669583690381448)
XLA Ops:
  0.0 29.3 %shard_map.118 = bf16[4,1024]{1,0:T(4,128)(2,1)} custom-call(bf16[4,2048]{1,0:T(4,128)(2,1)} %queries_hbm.1, bf16[4,1024]{1,0:T(4,128)(2,1)} %fresh_hbm.1, bf16[4,64,1024]{2,1,0:T(8,128)(2,1)} %kv_hbm.1, s32[4]{0:T(128)} %lengths_hbm.1, bf16[4,1024]{1,0:T(4,128)(2,1)} %residual_hbm.1, bf16[2048,1024]{1,0:T(8,128)(2,1)} %proj_hbm.1, f32[1,1024]{1,0:T(1,128)} %bitcast.4, ...), custom_call_target="tpu_custom_call" | custom-call | tf_op jit(solution)/shard_map/pallas_call | solution.py:677
  29.3 1.3 %copy.14 = bf16[4,1024]{1,0:T(4,128)(2,1)} copy(bf16[4,1024]{1,0:T(4,128)(2,1)} %shard_map.118) | data formatting | bytes 16384
